TPU v7x, 32 devices: a whole 2x2x4 slice. The times are simulated.
32 devices in a mesh: wide: 8 (over y, x, core), narrow: 4 (over z).
Axes of the slice: x: 2, y: 2, z: 4, core: 2. Of those that a mesh axis runs over, the one named last changes fastest.
Arguments:
- points: float32 [8, 16384], P(None, 'narrow'), may hold values from 0 to 1
- scales: float32 [8], replicated, may hold values from 2 to 6
- frequencies: float32 [8, 32768], P(None, 'wide'), may hold values from -24 to 24
- phases: float32 [32768], P('wide'), may hold values from -3.140625 to 3.140625
- feature_weights: bfloat16 [64, 32768], P(None, 'wide'), may hold values from -6 to 6
- targets: float32 [16384], P(('narrow', 'wide')), may hold values from -6 to 6
- noise: float32 [64, 16384], P(None, ('narrow', 'wide')), may hold values from -1.8 to 1.8
- inverses: float32 [2, 8192, 8192], P(None, 'wide', 'narrow'), may hold values from -0.01767767 to 1.0176777
- groups: int32 [2, 64], replicated, may hold values from 0 to 127, as said below
Outputs:
- residual: float32 [64, 16384], P(None, ('narrow', 'wide'))
- weights: float32 [2, 64, 8192], P(None, None, 'wide')
Inputs may be any that keep to these rules, and one draw needn't show every extreme that they name: All entries differ; each names the group of points g * 128 to g * 128 + 127. In every block, the entries n * 16 to (n + 1) * 16 - 1 name groups of narrow index n's points, that is groups n * 32 to (n + 1) * 32 - 1.
All inputs are finite; a program needn't handle non-finite values.
Results may differ from a plain program's by a relative error of at most 0.00065.
Values may be sent and summed in bfloat16 or wider, within the bound.
No kernel may reach another device: no remote copies, remote signals or barrier semaphores. Data moves between devices by JAX's collectives and lax.ppermute only.
A program may use at most 128 MiB of HBM per device.

v0:
```python
import math

import jax
import jax.numpy as jnp
from jax import lax
from jax.sharding import PartitionSpec as P

FEATURES = 32768
GROUP = 128
BLOCKS = 2


NOISE_VAR = 0.1
ROOT_FIVE = math.sqrt(5.0)
HIGH = lax.Precision.HIGHEST


def matern_tile(rows_coords, cols_coords, row_ids, col_ids):
    dist_sq = jnp.zeros((rows_coords.shape[1], cols_coords.shape[1]), jnp.float32)
    for coord in range(rows_coords.shape[0]):
        differ = rows_coords[coord][:, None] - cols_coords[coord][None, :]
        dist_sq = dist_sq + differ * differ
    scaled = ROOT_FIVE * jnp.sqrt(dist_sq)
    values = (1.0 + scaled + scaled * scaled / 3.0) * jnp.exp(-scaled)
    return values + jnp.where(row_ids[:, None] == col_ids[None, :], NOISE_VAR, 0.0)


def prior_terms(points_here, freq_part, phase_part, weights_part):
    width = points_here.shape[1]
    block = math.gcd(width, 1024)
    output = jnp.zeros((weights_part.shape[0], width), jnp.float32)

    def prior_one_block(index, output):
        begin = index * block
        coords = lax.dynamic_slice_in_dim(points_here, begin, block, 1)
        angles = (
            lax.dot_general(
                freq_part,
                coords,
                (((0,), (0,)), ((), ())),
                precision=HIGH,
                preferred_element_type=jnp.float32,
            )
            + phase_part[:, None]
        )
        features = jnp.cos(angles).astype(jnp.bfloat16)
        partial_sum = jnp.dot(weights_part, features, preferred_element_type=jnp.float32)
        return lax.dynamic_update_slice_in_dim(output, partial_sum, begin, 1)

    return lax.fori_loop(0, width // block, prior_one_block, output)


def kernel_terms(update, row_coords, row_ids, col_coords, col_ids):
    width = col_coords.shape[1]
    block = math.gcd(width, 2048)
    output = jnp.zeros((update.shape[0], width), jnp.float32)

    def kernel_one_block(index, output):
        begin = index * block
        tile = matern_tile(
            row_coords,
            lax.dynamic_slice_in_dim(col_coords, begin, block, 1),
            row_ids,
            lax.dynamic_slice_in_dim(col_ids, begin, block, 0),
        )
        product = jnp.dot(update, tile, precision=HIGH, preferred_element_type=jnp.float32)
        return lax.dynamic_update_slice_in_dim(output, product, begin, 1)

    return lax.fori_loop(0, width // block, kernel_one_block, output)


def spread_rows(residual):
    return lax.all_gather(residual, "wide", axis=1, tiled=True)


def on_device(
    points, scales, frequencies, phases, feature_weights, targets, noise, inverses, groups
):
    wide_count = lax.axis_size("wide")
    narrow_count = lax.axis_size("narrow")
    wide_here = lax.axis_index("wide")
    narrow_here = lax.axis_index("narrow")
    shard_width = points.shape[1]
    all_points = lax.all_gather(points, "narrow", axis=1, tiled=True)
    terms = prior_terms(points, frequencies, phases, feature_weights)
    prior = lax.psum_scatter(terms, "wide", scatter_dimension=1, tiled=True)
    residual = targets[None, :] - math.sqrt(2.0 / FEATURES) * prior - noise
    scaled_all = scales[:, None] * all_points
    scaled_own = lax.dynamic_slice_in_dim(scaled_all, narrow_here * shard_width, shard_width, 1)
    col_ids = narrow_here * shard_width + jnp.arange(shard_width, dtype=jnp.int32)
    slice_groups = groups.shape[1] // narrow_count
    row_groups = groups.shape[1] // wide_count
    shard_groups = shard_width // GROUP
    member_offsets = jnp.arange(GROUP, dtype=jnp.int32)
    whole = spread_rows(residual)
    weight_list = []
    for block_index in range(BLOCKS):
        block_groups = groups[block_index]
        col_groups = (
            lax.dynamic_slice_in_dim(block_groups, narrow_here * slice_groups, slice_groups, 0)
            - narrow_here * shard_groups
        )
        stacked = whole.reshape(whole.shape[0], shard_groups, GROUP)
        picked = jnp.take(stacked, col_groups, axis=1).reshape(whole.shape[0], slice_groups * GROUP)
        partial_sum = lax.dot_general(
            picked,
            inverses[block_index],
            (((1,), (1,)), ((), ())),
            precision=HIGH,
            preferred_element_type=jnp.float32,
        )
        update = lax.psum(partial_sum, "narrow")
        weight_list.append(update)
        row_group_ids = lax.dynamic_slice_in_dim(
            block_groups, wide_here * row_groups, row_groups, 0
        )
        row_ids = (row_group_ids[:, None] * GROUP + member_offsets[None, :]).reshape(-1)
        row_coords = jnp.take(scaled_all, row_ids, axis=1)
        terms = kernel_terms(update, row_coords, row_ids, scaled_own, col_ids)
        residual = residual - lax.psum_scatter(terms, "wide", scatter_dimension=1, tiled=True)
        if block_index + 1 < BLOCKS:
            whole = spread_rows(residual)
    return (residual, jnp.stack(weight_list))


def solution(mesh):
    in_specs = (
        P(None, "narrow"),
        P(),
        P(None, "wide"),
        P("wide"),
        P(None, "wide"),
        P(("narrow", "wide")),
        P(None, ("narrow", "wide")),
        P(None, "wide", "narrow"),
        P(),
    )
    out_specs = (P(None, ("narrow", "wide")), P(None, None, "wide"))
    return jax.shard_map(
        on_device, mesh=mesh, in_specs=in_specs, out_specs=out_specs, check_vma=False
    )
```

profile of v0, /device:TPU:0, one launch (start us, length us, event | category | flops | bytes accessed | tf_op | source)
XLA Modules:
  0.0 751.9 jit_solution(9740605828732380192)
XLA Ops:
  7.3 295.5 %while.41 = (s32[]{:T(128)}, f32[64,4096]{1,0:T(8,128)S(1)}, f32[8,4096]{1,0:T(8,128)}, f32[8,4096]{1,0:T(8,128)}, f32[4096]{0:T(1024)}, /*index=5*/bf16[64,4096...) while((s32[]{:T(128)}, f32[64,4096]{1,0:T(8,128)S(1)}, f32[8,4096]{1,0:T(8,128)}, ...), condition=%wide.region_1.0_spmd, body=%wide.region_0.0_spmd.sunk | while | flops 947912704 | bytes 19841208 | solution.py:50
  7.3 71.2 %cosine_convert_fusion.2 = bf16[1024,4096]{1,0:T(8,128)(2,1)S(1)} fusion(f32[8,4096]{1,0:T(8,128)} %get-tuple-element.728, f32[4096]{0:T(1024)} %get-tuple-element.729, f32[8,4096]{1,0:T(8,128)} %get-tuple-element.727, s32[]{:T(128)S(6)} %select_n.144), kind=kOutput, calls=%fused_computation.6.clone.2 | convolution fusion | flops 411041792 | bytes 8568836 | tf_op jit(solution)/shard_map/while/body/eval_jaxpr/dot_general | solution.py:37
  78.5 2.7 fusion.203
  81.2 71.2 %cosine_convert_fusion.2 = bf16[1024,4096]{1,0:T(8,128)(2,1)S(1)} fusion(f32[8,4096]{1,0:T(8,128)} %get-tuple-element.728, f32[4096]{0:T(1024)} %get-tuple-element.729, f32[8,4096]{1,0:T(8,128)} %get-tuple-element.727, s32[]{:T(128)S(6)} %select_n.144), kind=kOutput, calls=%fused_computation.6.clone.2 | convolution fusion | flops 411041792 | bytes 8568836 | tf_op jit(solution)/shard_map/while/body/eval_jaxpr/dot_general | solution.py:37
  152.4 2.7 fusion.203
  155.1 71.2 %cosine_convert_fusion.2 = bf16[1024,4096]{1,0:T(8,128)(2,1)S(1)} fusion(f32[8,4096]{1,0:T(8,128)} %get-tuple-element.728, f32[4096]{0:T(1024)} %get-tuple-element.729, f32[8,4096]{1,0:T(8,128)} %get-tuple-element.727, s32[]{:T(128)S(6)} %select_n.144), kind=kOutput, calls=%fused_computation.6.clone.2 | convolution fusion | flops 411041792 | bytes 8568836 | tf_op jit(solution)/shard_map/while/body/eval_jaxpr/dot_general | solution.py:37
  226.2 2.7 fusion.203
  228.9 71.2 %cosine_convert_fusion.2 = bf16[1024,4096]{1,0:T(8,128)(2,1)S(1)} fusion(f32[8,4096]{1,0:T(8,128)} %get-tuple-element.728, f32[4096]{0:T(1024)} %get-tuple-element.729, f32[8,4096]{1,0:T(8,128)} %get-tuple-element.727, s32[]{:T(128)S(6)} %select_n.144), kind=kOutput, calls=%fused_computation.6.clone.2 | convolution fusion | flops 411041792 | bytes 8568836 | tf_op jit(solution)/shard_map/while/body/eval_jaxpr/dot_general | solution.py:37
  300.1 2.7 fusion.203
  305.4 141.1 %all_gather.9 = f32[8,16384]{0,1:T(8,128)} all-gather(f32[8,4096]{0,1:T(8,128)S(1)} %copy.21), channel_id=1, replica_groups=mesh['wide'=8,'narrow'=4] {'narrow'}, dimensions={1}, use_global_device_ids=true | all-gather | bytes 655360 | tf_op jit(solution)/shard_map/all_gather | solution.py:84
  446.5 1.6 subtract_subtract_fusion
  448.6 5.8 broadcast_multiply_fusion
  454.6 7.5 gather_fusion
  462.3 1.7 constant_dynamic-slice_fusion.5
  464.0 9.7 %all-gather.3.cloned.1.call-done = f32[64,4096]{1,0:T(8,128)} async-done(((f32[64,512]{1,0:T(8,128)}), f32[64,4096]{1,0:T(8,128)}) %all-gather.3.cloned.1.call-update) | async-done | bytes 1048592 | tf_op jit(solution)/shard_map/all_gather | solution.py:73
  476.5 12.5 %fusion.149 = f32[64,1024]{1,0:T(8,128)} fusion(f32[2,1024,2048]{2,1,0:T(8,128)} %param.26, f32[16,64,128]{2,1,0:T(8,128)} %gather_fusion.1, pred[16]{0:T(512)(128)(4,1)S(1)} %get-tuple-element.482), kind=kOutput, calls=%fused_computation.149 | convolution fusion | flops 1610743808 | bytes 9175056 | tf_op jit(solution)/shard_map/dot_general | solution.py:105
  490.0 34.5 %all-reduce.3.cloned.1.call-done = f32[64,1024]{1,0:T(8,128)} async-done(((f32[64,1024]{1,0:T(8,128)}), f32[64,1024]{1,0:T(8,128)}) %all-reduce.3.cloned.1.call-update) | async-done | bytes 262160 | tf_op jit(solution)/shard_map/psum | solution.py:112
  524.5 35.2 %while.42 = (s32[]{:T(128)}, f32[64,4096]{1,0:T(8,128)S(1)}, f32[8,1024]{1,0:T(8,128)S(1)}, f32[8,4096]{1,0:T(8,128)S(1)}, s32[4096]{0:T(1024)S(1)}, /*index=5*/...) while((s32[]{:T(128)}, f32[64,4096]{1,0:T(8,128)S(1)}, ...), condition=%wide.region_5.8_spmd.clone, body=%wide.region_4.0_spmd.clone.sunk | while | flops 1679819776 | bytes 1114479 | solution.py:69
  525.0 17.0 %fusion.207 = f32[64,4096]{1,0:T(8,128)S(1)} fusion(f32[64,4096]{1,0:T(8,128)S(1)} %get-tuple-element.754, s32[]{:T(128)S(6)} %select_n.146, f32[64,1024]{1,0:T(8,128)} %get-tuple-element.776, s32[2048]{0:T(1024)S(1)} %dynamic_slice.94, f32[2048]{0:T(1024)S(1)} %bitcast.223, f32[1024]{0:T(1024)S(1)} %bitcast.233, f32[2048]{0:T(1024)S(1)} %bitcast.217, ...), kind=kOutput, calls=%fused_computation.71.clone.1 | convolution fusion | flops 1679818752 | bytes 897028 | tf_op jit(solution)/shard_map/while/body/eval_jaxpr/dot_general | solution.py:66
  542.4 17.0 %fusion.207 = f32[64,4096]{1,0:T(8,128)S(1)} fusion(f32[64,4096]{1,0:T(8,128)S(1)} %get-tuple-element.754, s32[]{:T(128)S(6)} %select_n.146, f32[64,1024]{1,0:T(8,128)} %get-tuple-element.776, s32[2048]{0:T(1024)S(1)} %dynamic_slice.94, f32[2048]{0:T(1024)S(1)} %bitcast.223, f32[1024]{0:T(1024)S(1)} %bitcast.233, f32[2048]{0:T(1024)S(1)} %bitcast.217, ...), kind=kOutput, calls=%fused_computation.71.clone.1 | convolution fusion | flops 1679818752 | bytes 897028 | tf_op jit(solution)/shard_map/while/body/eval_jaxpr/dot_general | solution.py:66
  560.9 35.9 %reduce-scatter.6.cloned.1.call-done = f32[64,512]{1,0:T(8,128)} async-done(((f32[64,4096]{1,0:T(8,128)}), f32[64,512]{1,0:T(8,128)}) %reduce-scatter.6.cloned.1.call-update) | async-done | bytes 131088 | tf_op jit(solution)/shard_map/reduce_scatter | solution.py:120
  596.8 1.6 sub.695
  598.7 24.1 %all-gather.5.cloned.1.call-done = f32[64,4096]{1,0:T(8,128)} async-done(((f32[64,512]{1,0:T(8,128)}), f32[64,4096]{1,0:T(8,128)}) %all-gather.5.cloned.1.call-update) | async-done | bytes 1048592 | tf_op jit(solution)/shard_map/all_gather | solution.py:73
  624.7 11.3 %fusion.147 = f32[64,1024]{1,0:T(8,128)} fusion(f32[2,1024,2048]{2,1,0:T(8,128)} %param.26, f32[16,64,128]{2,1,0:T(8,128)S(1)} %gather_fusion.3, pred[16]{0:T(512)(128)(4,1)S(1)} %get-tuple-element.480), kind=kOutput, calls=%fused_computation.147 | convolution fusion | flops 1610743808 | bytes 9175056 | tf_op jit(solution)/shard_map/dot_general | solution.py:105
  636.1 6.2 gather_fusion.2
  642.7 28.8 %all-reduce.5.cloned.1.call-done = f32[64,1024]{1,0:T(8,128)} async-done(((f32[64,1024]{1,0:T(8,128)}), f32[64,1024]{1,0:T(8,128)}) %all-reduce.5.cloned.1.call-update) | async-done | bytes 262160 | tf_op jit(solution)/shard_map/psum | solution.py:112
  671.6 34.8 %while.43 = (s32[]{:T(128)}, f32[64,4096]{1,0:T(8,128)S(1)}, f32[8,1024]{1,0:T(8,128)S(1)}, f32[8,4096]{1,0:T(8,128)S(1)}, s32[4096]{0:T(1024)S(1)}, /*index=5*/...) while((s32[]{:T(128)}, f32[64,4096]{1,0:T(8,128)S(1)}, ...), condition=%wide.region_9.12_spmd.clone, body=%wide.region_8.11_spmd.clone.sunk | while | flops 1679819776 | bytes 1114479 | solution.py:69
  672.1 17.0 %fusion.211 = f32[64,4096]{1,0:T(8,128)S(1)} fusion(f32[64,4096]{1,0:T(8,128)S(1)} %get-tuple-element.808, s32[]{:T(128)S(6)} %select_n.148, f32[64,1024]{1,0:T(8,128)} %get-tuple-element.830, s32[2048]{0:T(1024)S(1)} %dynamic_slice.95, f32[2048]{0:T(1024)S(1)} %bitcast.231, f32[1024]{0:T(1024)S(1)} %bitcast.241, f32[2048]{0:T(1024)S(1)} %bitcast.225, ...), kind=kOutput, calls=%fused_computation.139.clone.1 | convolution fusion | flops 1679818752 | bytes 897028 | tf_op jit(solution)/shard_map/while/body/eval_jaxpr/dot_general | solution.py:66
  689.4 17.0 %fusion.211 = f32[64,4096]{1,0:T(8,128)S(1)} fusion(f32[64,4096]{1,0:T(8,128)S(1)} %get-tuple-element.808, s32[]{:T(128)S(6)} %select_n.148, f32[64,1024]{1,0:T(8,128)} %get-tuple-element.830, s32[2048]{0:T(1024)S(1)} %dynamic_slice.95, f32[2048]{0:T(1024)S(1)} %bitcast.231, f32[1024]{0:T(1024)S(1)} %bitcast.241, f32[2048]{0:T(1024)S(1)} %bitcast.225, ...), kind=kOutput, calls=%fused_computation.139.clone.1 | convolution fusion | flops 1679818752 | bytes 897028 | tf_op jit(solution)/shard_map/while/body/eval_jaxpr/dot_general | solution.py:66
  707.4 1.8 pad_maximum_fusion
  709.2 34.1 %reduce-scatter.8.cloned.1.call-done = f32[64,512]{1,0:T(8,128)} async-done(((f32[64,4096]{1,0:T(8,128)}), f32[64,512]{1,0:T(8,128)}) %reduce-scatter.8.cloned.1.call-update) | async-done | bytes 131088 | tf_op jit(solution)/shard_map/reduce_scatter | solution.py:120
  743.3 1.6 sub.698
  (86 shorter events, 13.6 us)
Async XLA Ops:
  7.2 439.3 %reduce-scatter.4.cloned.1.call-start = ((), (), s32[]{:S(2)}) async-start(), calls=%async_computation.3 | async-start | bytes 1179648 | tf_op jit(solution)/shard_map/reduce_scatter | solution.py:86
  7.3 71.2 %copy-start = (bf16[64,4096]{1,0:T(8,128)(2,1)S(1)}, bf16[64,4096]{1,0:T(8,128)(2,1)}, u32[]{:S(2)}) copy-start(bf16[64,4096]{1,0:T(8,128)(2,1)} %get-tuple-element.730) | copy-start | bytes 1572868 | tf_op jit(solution)/shard_map/while
  81.2 71.2 %copy-start = (bf16[64,4096]{1,0:T(8,128)(2,1)S(1)}, bf16[64,4096]{1,0:T(8,128)(2,1)}, u32[]{:S(2)}) copy-start(bf16[64,4096]{1,0:T(8,128)(2,1)} %get-tuple-element.730) | copy-start | bytes 1572868 | tf_op jit(solution)/shard_map/while
  155.0 71.2 %copy-start = (bf16[64,4096]{1,0:T(8,128)(2,1)S(1)}, bf16[64,4096]{1,0:T(8,128)(2,1)}, u32[]{:S(2)}) copy-start(bf16[64,4096]{1,0:T(8,128)(2,1)} %get-tuple-element.730) | copy-start | bytes 1572868 | tf_op jit(solution)/shard_map/while
  228.9 71.2 %copy-start = (bf16[64,4096]{1,0:T(8,128)(2,1)S(1)}, bf16[64,4096]{1,0:T(8,128)(2,1)}, u32[]{:S(2)}) copy-start(bf16[64,4096]{1,0:T(8,128)(2,1)} %get-tuple-element.730) | copy-start | bytes 1572868 | tf_op jit(solution)/shard_map/while
  302.8 1.1 copy-start.2
  302.8 143.7 %copy-start.8 = (f32[64,512]{1,0:T(8,128)S(1)}, f32[64,512]{1,0:T(8,128)}, u32[]{:S(2)}) copy-start(f32[64,512]{1,0:T(8,128)} %param.25) | copy-start | bytes 393220
  302.8 143.7 %copy-start.9 = (f32[512]{0:T(512)S(1)}, f32[512]{0:T(512)}, u32[]{:S(2)}) copy-start(f32[512]{0:T(512)} %param.24) | copy-start | bytes 6148
  302.8 145.8 %copy-start.11 = (f32[8]{0:T(128)S(1)}, f32[8]{0:T(128)}, u32[]{:S(2)}) copy-start(f32[8]{0:T(128)} %param.20) | copy-start | bytes 100
  303.9 169.8 %all-gather.3.cloned.1.call-start = ((), (), s32[]{:S(2)}) async-start(), calls=%async_computation.4 | async-start | bytes 1179648 | tf_op jit(solution)/shard_map/all_gather | solution.py:73
  448.1 6.3 copy-start.10
  448.1 76.3 %all-reduce.3.cloned.1.call-start = ((), (), s32[]{:S(2)}) async-start(), calls=%async_computation.5 | async-start | bytes 524288 | tf_op jit(solution)/shard_map/psum | solution.py:112
  476.5 12.5 %copy-start.6 = (f32[1024,8]{1,0:T(8,128)S(1)}, f32[1024,8]{1,0:T(8,128)}, u32[]{:S(2)}) copy-start(f32[1024,8]{1,0:T(8,128)} %gather_fusion) | copy-start | bytes 98308
  489.0 107.8 %reduce-scatter.6.cloned.1.call-start = ((), (), s32[]{:S(2)}) async-start(), calls=%async_computation.6 | async-start | bytes 1179648 | tf_op jit(solution)/shard_map/reduce_scatter | solution.py:120
  524.5 72.3 %copy-start.4 = (f32[64,512]{1,0:T(8,128)S(1)}, f32[64,512]{1,0:T(8,128)}, u32[]{:S(2)}) copy-start(f32[64,512]{1,0:T(8,128)} %subtract_subtract_fusion) | copy-start | bytes 393220
  559.7 1.1 copy-start.3
  560.8 61.9 %all-gather.5.cloned.1.call-start = ((), (), s32[]{:S(2)}) async-start(), calls=%async_computation.7 | async-start | bytes 1179648 | tf_op jit(solution)/shard_map/all_gather | solution.py:73
  598.4 73.1 %all-reduce.5.cloned.1.call-start = ((), (), s32[]{:S(2)}) async-start(), calls=%async_computation.8 | async-start | bytes 524288 | tf_op jit(solution)/shard_map/psum | solution.py:112
  636.0 107.3 %reduce-scatter.8.cloned.1.call-start = ((), (), s32[]{:S(2)}) async-start(), calls=%async_computation.9 | async-start | bytes 1179648 | tf_op jit(solution)/shard_map/reduce_scatter | solution.py:120
  671.5 35.9 %copy-start.7 = (f32[64,1024]{1,0:T(8,128)S(1)}, f32[64,1024]{1,0:T(8,128)}, u32[]{:S(2)}) copy-start(f32[64,1024]{1,0:T(8,128)} %get-tuple-element.869) | copy-start | bytes 786436
  671.5 71.8 %copy-start.5 = (f32[64,512]{1,0:T(8,128)S(1)}, f32[64,512]{1,0:T(8,128)}, u32[]{:S(2)}) copy-start(f32[64,512]{1,0:T(8,128)} %sub.695) | copy-start | bytes 393220
  706.4 1.0 copy-start.1
Sparse Core Ops, SparseCore 0:
  304.0 38.7 reduce-scatter.3
  448.2 25.4 all-gather.2
  489.1 35.3 all-reduce.2
  560.9 35.7 reduce-scatter.5
  599.3 23.4 all-gather.4
  636.1 35.2 all-reduce.4
  707.5 35.7 reduce-scatter.7
where the time goes:
time: 758 us; the launch traced here: 752 us
  matrix products  387 us (51%)
  waiting for transfers between devices  167 us (22%)
  blocking collectives  141 us (19%)
  local copies, waits for them, and re-layouts  26.8 us (4%)
  between operations  14.5 us (2%)
  other arithmetic  13.6 us (2%)
    dot_general x4, matrix products, prior_one_block(): lax.dot_general(freq_part, coords, (((0,), (0,)), ((), ())), precision=HI...  285 us
    all_gather x1, blocking collectives, on_device(): all_points = lax.all_gather(points, 'narrow', axis=1, tiled=True)  141 us
    reduce_scatter x2, waiting for transfers between devices, on_device(): lax.psum_scatter(terms, 'wide', scatter_dimension=1, tiled=True)  70 us
    dot_general x4, matrix products, kernel_one_block(): jnp.dot(update, tile, precision=HIGH, preferred_element_type=jnp.float32)  67.8 us
    psum x2, waiting for transfers between devices, on_device(): update = lax.psum(partial_sum, 'narrow')  63.2 us
    all_gather x2, waiting for transfers between devices, spread_rows(): return lax.all_gather(residual, 'wide', axis=1, tiled=True)  33.8 us
    dot_general x2, matrix products, on_device(): lax.dot_general(picked, inverses[block_index], (((1,), (1,)), ((), ())),...  23.7 us
  transfers between devices with their start and end apart: 7, of which 6 were waited for; matrix products, arithmetic and copies ran while one was open for 4% of the time, Pallas kernels for 0%

commit v1 on v0

v1 whole, which is shorter than its diff:
```python
import functools
import math

import jax
import jax.numpy as jnp
from jax import lax
from jax.experimental import pallas as pl
from jax.experimental.pallas import tpu as pltpu
from jax.sharding import PartitionSpec as P

GROUP = 128
BLOCKS = 2
NOISE_VAR = 0.1
LN2 = math.log(2.0)
TO_TURNS = 1.0 / (2.0 * math.pi)
TO_U = math.sqrt(5.0) / LN2
SINE = (-6.283164044164058, 41.33714235333657, -81.34076831835199, 70.99342806157215)
VMEM = 44 << 20
F32 = jnp.float32
BF16 = jnp.bfloat16


def thirds(x):
    high = x.astype(BF16).astype(F32)
    rest = x - high
    mid = rest.astype(BF16).astype(F32)
    low = (rest - mid).astype(BF16).astype(F32)
    return high, mid, low


def halves(x):
    high = x.astype(BF16)
    return high, (x - high.astype(F32)).astype(BF16)


def stack_rows(rows):
    width = max(row.shape[1] for row in rows)
    at = lax.broadcasted_iota(jnp.int32, (8, width), 0)
    out = jnp.zeros((8, width), F32)
    for index, row in enumerate(rows):
        out = jnp.where(at == index, row, out)
    return out


def left_terms(parts, extra):
    high, mid, low = parts
    return jnp.concatenate([high, high, mid, mid, high, low, extra, jnp.zeros_like(high)], 0)


def right_terms(parts, extra):
    high, mid, low = parts
    return jnp.concatenate([high, mid, high, mid, low, high, extra, jnp.zeros_like(high)], 0)


def cosine(turns):
    fraction = turns - jnp.round(turns)
    shifted = jnp.abs(fraction) - 0.25
    square = shifted * shifted
    value = SINE[-1]
    for factor in SINE[-2::-1]:
        value = value * square + factor
    return value * shifted


def group_of(ref, index):
    return ref[:, pl.ds(pl.multiple_of(index * GROUP, GROUP), GROUP)]


def whole_block(array):
    return pl.BlockSpec(array.shape, lambda i, *_: (0,) * array.ndim)


def prior_body(
    tile, chunk, own, factor, order, place, freq, phase, fw, points, targets, noise, out, left
):
    features = freq.shape[1]

    @pl.when(pl.program_id(0) == 0)
    def _():
        step = math.gcd(features, 512)
        for begin in range(0, features, step):
            cut = slice(begin, begin + step)
            extra = stack_rows(thirds(phase[:, cut] * TO_TURNS))
            terms = left_terms(thirds(freq[:, cut] * TO_TURNS), extra)
            left[cut, :] = terms.T.astype(BF16)

    per = tile // GROUP
    first = pl.program_id(0) * per
    coords = jnp.concatenate([group_of(points, order[first + k]) for k in range(per)], 1)
    ones = jnp.ones((1, tile), F32)
    right = right_terms(thirds(coords), stack_rows([ones] * 3)).astype(BF16)
    total = jnp.zeros(out.shape, F32)
    for begin in range(0, features, chunk):
        turns = jnp.dot(left[begin : begin + chunk, :], right, preferred_element_type=F32)
        values = cosine(turns).astype(BF16)
        total += jnp.dot(fw[:, begin : begin + chunk], values, preferred_element_type=F32)
    out[...] = -factor * total
    for k in range(per):
        group = order[first + k]

        @pl.when(group // own == place[0])
        def _():
            inside = lax.rem(group, own)
            cut = slice(k * GROUP, (k + 1) * GROUP)
            out[:, cut] += group_of(targets, inside) - group_of(noise, inside)


def prior_part(order, place, own, factor, freq, phase, fw, points, targets, noise, name):
    samples, features = fw.shape
    width = order.shape[0] * GROUP
    tile = math.gcd(width, 512)
    body = functools.partial(prior_body, tile, math.gcd(features, 2048), own, factor)
    arrays = (freq, phase, fw, points, targets, noise)
    return pl.pallas_call(
        body,
        out_shape=jax.ShapeDtypeStruct((samples, width), F32),
        grid_spec=pltpu.PrefetchScalarGridSpec(
            num_scalar_prefetch=2,
            grid=(width // tile,),
            in_specs=[whole_block(array) for array in arrays],
            out_specs=pl.BlockSpec((samples, tile), lambda i, *_: (0, i)),
            scratch_shapes=[pltpu.VMEM((features, 64), BF16)],
        ),
        compiler_params=pltpu.CompilerParams(vmem_limit_bytes=VMEM),
        cost_estimate=pl.CostEstimate(
            flops=14 * features * width + 2 * (samples + 64) * features * width,
            bytes_accessed=samples * (2 * features + 4 * width),
            transcendentals=features * width,
        ),
        name=name,
    )(order, place, *arrays)


def inverse_body(x, inverse, out, terms):
    samples = x.shape[0]

    @pl.when(pl.program_id(0) == 0)
    def _():
        high, low = halves(x[...])
        terms[:samples, :] = high
        terms[samples:, :] = low

    high, low = halves(inverse[...])
    dims = (((1,), (1,)), ((), ()))
    both = lax.dot_general(terms[...], high, dims, preferred_element_type=F32)
    rest = lax.dot_general(terms[:samples, :], low, dims, preferred_element_type=F32)
    out[...] = both[:samples] + both[samples:] + rest


def inverse_part(x, inverses, block, name):
    samples, depth = x.shape
    rows = inverses.shape[1]
    tile = math.gcd(rows, 256)
    return pl.pallas_call(
        inverse_body,
        out_shape=jax.ShapeDtypeStruct((samples, rows), F32),
        grid=(rows // tile,),
        in_specs=[
            whole_block(x),
            pl.BlockSpec((None, tile, depth), lambda i: (block, i, 0)),
        ],
        out_specs=pl.BlockSpec((samples, tile), lambda i: (0, i)),
        scratch_shapes=[pltpu.VMEM((2 * samples, depth), BF16)],
        compiler_params=pltpu.CompilerParams(vmem_limit_bytes=VMEM),
        cost_estimate=pl.CostEstimate(
            flops=6 * samples * rows * depth, bytes_accessed=4 * rows * depth, transcendentals=0
        ),
        name=name,
    )(x, inverses)


def kernel_coords(coords, scales):
    centred = (coords - 0.5) * (scales * TO_U)
    return centred, jnp.sum(centred * centred, axis=0, keepdims=True)


def kernel_body(
    tile, start, block, own, shuffle, order, rows, place, every, scales, update, carry, out, left, terms
):
    samples = update.shape[0]
    groups = rows.shape[0]

    @pl.when(pl.program_id(0) == 0)
    def _():
        for j in range(groups):
            group = rows[j]
            owner, inside = group // place[3], lax.rem(group, place[3])
            coords = every[owner, :, pl.ds(pl.multiple_of(inside * GROUP, GROUP), GROUP)]
            centred, norm = kernel_coords(coords, scales[...])
            ones = jnp.ones((1, GROUP), F32)
            extra = stack_rows([*thirds(norm), ones, ones, ones])
            matrix = left_terms([-2.0 * part for part in thirds(centred)], extra)
            left[j * GROUP : (j + 1) * GROUP, :] = matrix.T.astype(BF16)
        high, low = halves(update[...])
        terms[:samples, :] = high
        terms[samples:, :] = low

    per = tile // GROUP
    first = pl.program_id(0) * per
    coords = jnp.concatenate(
        [
            every[place[1], :, pl.ds(pl.multiple_of(order[first + k] * GROUP, GROUP), GROUP)]
            for k in range(per)
        ],
        1,
    )
    centred, norm = kernel_coords(coords, scales[...])
    ones = jnp.ones((1, tile), F32)
    right = right_terms(thirds(centred), stack_rows([ones, ones, ones, *thirds(norm)])).astype(BF16)
    square = jnp.dot(left[...], right, preferred_element_type=F32)
    square = jnp.maximum(square, 1e-20)
    u = square * lax.rsqrt(square)
    values = (1.0 + u * (LN2 + (LN2 * LN2 / 3.0) * u)) * jnp.exp2(-u)
    high, low = halves(values)
    both = jnp.dot(terms[...], high, preferred_element_type=F32)
    rest = jnp.dot(terms[:samples, :], low, preferred_element_type=F32)
    total = both[:samples] + both[samples:] + rest
    for k in range(per):
        entry = first + k + start - block * place[2]
        row = place[1] * place[2] + entry - place[0] * groups
        mine = (entry >= 0) & (entry < place[2]) & (row >= 0) & (row < groups)
        weight = jnp.where(mine, NOISE_VAR, 0.0)
        cut = slice(k * GROUP, (k + 1) * GROUP)
        diagonal = group_of(update, jnp.clip(row, 0, groups - 1))
        value = carry[:, cut] - total[:, cut] - weight * diagonal
        if shuffle:
            group = order[first + k]
            inside = pl.multiple_of(lax.rem(group, own) * GROUP, GROUP)
            out[group // own, :, pl.ds(inside, GROUP)] = value
        else:
            out[:, cut] = value


def kernel_part(order, rows, place, every, scales, update, carry, start, block, own, shuffle, name):
    samples = update.shape[0]
    width = order.shape[0] * GROUP
    tile = math.gcd(width, 256)
    parts = width // (own * GROUP)
    shape = (parts, samples, own * GROUP) if shuffle else (samples, width)
    if shuffle:
        out_spec = pl.BlockSpec(shape, lambda i, *_: (0, 0, 0))
    else:
        out_spec = pl.BlockSpec((samples, tile), lambda i, *_: (0, i))
    depth = rows.shape[0] * GROUP
    return pl.pallas_call(
        functools.partial(kernel_body, tile, start, block, own, shuffle),
        out_shape=jax.ShapeDtypeStruct(shape, F32),
        grid_spec=pltpu.PrefetchScalarGridSpec(
            num_scalar_prefetch=3,
            grid=(width // tile,),
            in_specs=[
                whole_block(every),
                whole_block(scales),
                whole_block(update),
                pl.BlockSpec((samples, tile), lambda i, *_: (0, i)),
            ],
            out_specs=out_spec,
            scratch_shapes=[
                pltpu.VMEM((depth, 64), BF16),
                pltpu.VMEM((2 * samples, depth), BF16),
            ],
        ),
        compiler_params=pltpu.CompilerParams(vmem_limit_bytes=VMEM),
        cost_estimate=pl.CostEstimate(
            flops=14 * depth * width + 6 * (samples + 20) * depth * width,
            bytes_accessed=8 * samples * width,
            transcendentals=2 * depth * width,
        ),
        name=name,
    )(order, rows, place, every, scales, update, carry)


def exchange(value, axis, mask):
    count = lax.axis_size(axis)
    return lax.ppermute(value, axis, [(i, i ^ mask) for i in range(count)])


def butterfly(value, axis, masks):
    if not masks:
        return value
    if len(masks) == 1:
        return value + exchange(value, axis, masks[0])
    rows = value.shape[0] // 2
    upper, lower = value[:rows], value[rows:]
    turned = masks[1:] + masks[:1]
    for one, two in zip(masks, turned):
        got_upper, got_lower = exchange(upper, axis, one), exchange(lower, axis, two)
        upper, lower = upper + got_upper, lower + got_lower
    return jnp.concatenate([upper, lower], 0)


def sum_wide(value):
    count = lax.axis_size("wide")
    if count & (count - 1) or count < 2:
        return lax.psum(value, "wide")
    core = lax.rem(lax.axis_index("wide"), 2)
    rows = value.shape[0] // 2
    mine = lax.dynamic_slice_in_dim(value, core * rows, rows, 0)
    other = lax.dynamic_slice_in_dim(value, (1 - core) * rows, rows, 0)
    summed = mine + exchange(other, "wide", 1)
    summed = butterfly(summed, "wide", [1 << bit for bit in range(1, count.bit_length() - 1)])
    got = exchange(summed, "wide", 1)
    first = core == 0
    return jnp.concatenate([jnp.where(first, summed, got), jnp.where(first, got, summed)], 0)


def sum_narrow(value):
    count = lax.axis_size("narrow")
    if count & (count - 1):
        return lax.psum(value, "narrow")
    return butterfly(value, "narrow", [(2 << bit) - 1 for bit in range(count.bit_length() - 1)])


def scatter_wide(parts):
    count = lax.axis_size("wide")
    here = lax.axis_index("wide")
    if count & (count - 1) or count < 2:
        return lax.psum_scatter(parts, "wide", scatter_dimension=0, tiled=False)
    core, chip = lax.rem(here, 2), here // 2
    pairs = parts.reshape(count // 2, 2, *parts.shape[1:])
    mine = lax.dynamic_slice_in_dim(pairs, core, 1, 1)[:, 0]
    other = lax.dynamic_slice_in_dim(pairs, 1 - core, 1, 1)[:, 0]
    summed = mine + exchange(other, "wide", 1)

    def pick(mask):
        return lax.dynamic_slice_in_dim(summed, chip ^ mask, 1, 0)[0]

    got = [exchange(pick(mask), "wide", 2 * mask) for mask in range(1, count // 2)]
    return sum(got, pick(0))


def order_of_groups(local, total):
    used = local.reshape(-1)
    if used.shape[0] == total:
        return used
    ids = jnp.arange(total, dtype=jnp.int32)
    taken = jnp.any(ids[:, None] == used[None, :], axis=1)
    before = (ids[None, :] < ids[:, None]) & ~taken[None, :]
    spot = used.shape[0] + jnp.sum(before.astype(jnp.int32), axis=1)
    slots = jnp.arange(used.shape[0], total, dtype=jnp.int32)
    hit = (spot[None, :] == slots[:, None]) & ~taken[None, :]
    others = jnp.sum(jnp.where(hit, ids[None, :], 0), axis=1).astype(jnp.int32)
    return jnp.concatenate([used, others])


def on_device(
    all_features,
    points,
    scales,
    frequencies,
    phases,
    feature_weights,
    targets,
    noise,
    inverses,
    groups,
):
    wide_count = lax.axis_size("wide")
    narrow_count = lax.axis_size("narrow")
    wide_here = lax.axis_index("wide").astype(jnp.int32)
    narrow_here = lax.axis_index("narrow").astype(jnp.int32)
    shard_groups = points.shape[1] // GROUP
    own = shard_groups // wide_count
    slice_groups = groups.shape[1] // narrow_count
    row_groups = groups.shape[1] // wide_count
    place = jnp.stack(
        [wide_here, narrow_here, jnp.int32(slice_groups), jnp.int32(shard_groups)]
    )
    every = lax.all_gather(points, "narrow", axis=0, tiled=False)
    local = lax.dynamic_slice_in_dim(groups, narrow_here * slice_groups, slice_groups, 1)
    order = order_of_groups(local - narrow_here * shard_groups, shard_groups)
    rows = lax.dynamic_slice_in_dim(groups, wide_here * row_groups, row_groups, 1)
    cuts = [order[:slice_groups], order[slice_groups : 2 * slice_groups], order[2 * slice_groups :]]
    width = slice_groups * GROUP

    prior = functools.partial(
        prior_part,
        place=place,
        own=own,
        factor=math.sqrt(2.0 / all_features),
        freq=frequencies,
        phase=phases[None, :],
        fw=feature_weights,
        points=points,
        targets=targets[None, :],
        noise=noise,
    )
    first = prior(order[:slice_groups], name="prior_first")
    whole = sum_wide(first)
    later = prior(order[slice_groups:], name="prior_later")
    part = inverse_part(whole, inverses, 0, "inverse_0")
    update = sum_narrow(part)
    term = functools.partial(
        kernel_part, place=place, every=every, scales=scales[:, None], own=own
    )
    term_0 = functools.partial(term, rows=rows[0], update=update, block=0, shuffle=False)
    middle = term_0(cuts[1], carry=later[:, :width], start=slice_groups, name="kernel_0_next")
    whole = sum_wide(middle)
    done = [term_0(cuts[0], carry=first, start=0, name="kernel_0_own"), middle]
    if cuts[2].shape[0]:
        done.append(
            term_0(cuts[2], carry=later[:, width:], start=2 * slice_groups, name="kernel_0_rest")
        )
    carry = jnp.concatenate(done, 1)
    part = inverse_part(whole, inverses, 1, "inverse_1")
    update_1 = sum_narrow(part)
    parts = term(
        order,
        rows=rows[1],
        update=update_1,
        carry=carry,
        start=0,
        block=1,
        shuffle=True,
        name="kernel_1",
    )
    return scatter_wide(parts), jnp.stack([update, update_1])


def solution(mesh):
    in_specs = (
        P(None, "narrow"),
        P(),
        P(None, "wide"),
        P("wide"),
        P(None, "wide"),
        P(("narrow", "wide")),
        P(None, ("narrow", "wide")),
        P(None, "wide", "narrow"),
        P(),
    )
    out_specs = (P(None, ("narrow", "wide")), P(None, None, "wide"))

    def run(points, scales, frequencies, *others):
        return jax.shard_map(
            functools.partial(on_device, frequencies.shape[1]),
            mesh=mesh,
            in_specs=in_specs,
            out_specs=out_specs,
            check_vma=False,
        )(points, scales, frequencies, *others)

    return run
```

time: 758 us -> 165 us (0.22)
  matrix products: 387 us -> 0 us
  waiting for transfers between devices: 167 us -> 32.3 us
  blocking collectives: 141 us -> 17.7 us
  Pallas kernels: 0 us -> 77.3 us
  starting transfers between devices: 0.75 us -> 27.2 us
  local copies, waits for them, and re-layouts: 26.8 us -> 5.64 us
  between operations: 14.5 us -> 1.05 us
  other arithmetic: 13.6 us -> 3.18 us
    dot_general x14 -> x0, matrix products: 387 us -> none  [the longest x4 285 us: prior_one_block(): lax.dot_general(freq_part, coords, (((0,), (0,)), ((), ())), precision=HI...]
    all_gather x1, blocking collectives: 141 us -> 17.7 us  [on_device(): every = lax.all_gather(points, 'narrow', axis=0, tiled=False)]
    pallas_call x0 -> x7, Pallas kernels: none -> 77.3 us  [the longest x2 33.4 us: prior_part(): pl.pallas_call(body, out_shape=jax.ShapeDtypeStruct((samples, width), F32...]
    reduce_scatter x3 -> x0, waiting for transfers between devices: 70 us -> none  [the longest x2 70 us: on_device(): lax.psum_scatter(terms, 'wide', scatter_dimension=1, tiled=True)]
    psum x2 -> x0, waiting for transfers between devices: 63.2 us -> none  [on_device(): update = lax.psum(partial_sum, 'narrow')]
    all_gather x2 -> x0, waiting for transfers between devices: 33.8 us -> none  [spread_rows(): return lax.all_gather(residual, 'wide', axis=1, tiled=True)]
    ppermute x0 -> x24, waiting for transfers between devices: none -> 32.3 us  [exchange(): return lax.ppermute(value, axis, [(i, i ^ mask) for i in range(count)])]
    ppermute x0 -> x24, starting transfers between devices: none -> 27.2 us  [exchange(): return lax.ppermute(value, axis, [(i, i ^ mask) for i in range(count)])]
  transfers between devices with their start and end apart: 7 -> 24, of which waited for: 6 -> 18; matrix products, arithmetic and copies ran while one was open for 4% -> 1% of each run, Pallas kernels for 0% -> 15%
where the time goes in v1:
time: 165 us; the launch traced here: 164 us
  Pallas kernels  77.3 us (47%)
  waiting for transfers between devices  32.3 us (20%)
  starting transfers between devices  27.2 us (16%)
  blocking collectives  17.7 us (11%)
  local copies, waits for them, and re-layouts  5.64 us (3%)
  other arithmetic  3.18 us (2%)
    pallas_call x2, Pallas kernels, prior_part(): pl.pallas_call(body, out_shape=jax.ShapeDtypeStruct((samples, width), F32...  33.4 us
    pallas_call x3, Pallas kernels, kernel_part(): pl.pallas_call(functools.partial(kernel_body, tile, start, block, own, sh...  32.3 us
    ppermute x24, waiting for transfers between devices, exchange(): return lax.ppermute(value, axis, [(i, i ^ mask) for i in range(count)])  32.3 us
    ppermute x24, starting transfers between devices, exchange(): return lax.ppermute(value, axis, [(i, i ^ mask) for i in range(count)])  27.2 us
    all_gather x1, blocking collectives, on_device(): every = lax.all_gather(points, 'narrow', axis=0, tiled=False)  17.7 us
    pallas_call x2, Pallas kernels, inverse_part(): pl.pallas_call(inverse_body, out_shape=jax.ShapeDtypeStruct((samples, row...  11.5 us
    unnamed x26, local copies, waits for them, and re-layouts  5.18 us
  transfers between devices with their start and end apart: 24, of which 18 were waited for; matrix products, arithmetic and copies ran while one was open for 1% of the time, Pallas kernels for 15%

profile of v1, /device:TPU:0, one launch (start us, length us, event | category | flops | bytes accessed | tf_op | source)
XLA Modules:
  0.0 164.3 jit_solution(8253290647984991889)
XLA Ops:
  6.7 16.7 %prior_first.1.carry = f32[64,2048]{1,0:T(8,128)S(1)} custom-call(s32[16]{0:T(128)S(1)} %get-tuple-element.29.order, s32[4]{0:T(128)S(1)} %pad_add_fusion.place, f32[8,4096]{1,0:T(8,128)S(1)} %copy-done.4, f32[1,4096]{1,0:T(1,128)S(1)} %bitcast.40, bf16[64,4096]{1,0:T(8,128)(2,1)S(1)} %copy-done.2, f32[8,4096]{1,0:T(8,128)S(1)} %copy-done, ...), custom_call_target="tpu_custom_call" | custom-call | flops 2264924160 | bytes 1048576 | tf_op jit(solution)/shard_map/prior_first/pallas_call | solution.py:114
  25.2 2.9 %collective-permute-start.1 = (f32[16,2048]{1,0:T(8,128)S(1)}, f32[16,2048]{1,0:T(8,128)S(1)}, u32[]{:S(2)}, u32[]{:S(2)}) collective-permute-start(f32[16,2048]{1,0:T(8,128)S(1)} %get-tuple-element.27), channel_id=1, source_target_pairs={{0,8},{4,12},{8,0},{12,4},{16,24},{20,28},{24,16},{28,20},{1,9},{5... | collective-permute-start | bytes 393224 | tf_op jit(solution)/shard_map/ppermute | solution.py:275
  28.1 1.5 collective-permute-start.3
  29.6 2.3 %collective-permute-done.1 = f32[16,2048]{1,0:T(8,128)S(1)} collective-permute-done((f32[16,2048]{1,0:T(8,128)S(1)}, f32[16,2048]{1,0:T(8,128)S(1)}, u32[]{:S(2)}, u32[]{:S(2)}) %collective-permute-start.1) | collective-permute-done | bytes 131104 | tf_op jit(solution)/shard_map/ppermute | solution.py:275
  31.9 1.5 collective-permute-done.3
  33.8 1.7 %collective-permute-start.2 = (f32[16,2048]{1,0:T(8,128)S(1)}, f32[16,2048]{1,0:T(8,128)S(1)}, u32[]{:S(2)}, u32[]{:S(2)}) collective-permute-start(f32[16,2048]{1,0:T(8,128)S(1)} %get-tuple-element.25), channel_id=1, source_target_pairs={{0,16},{4,20},{8,24},{12,28},{16,0},{20,4},{24,8},{28,12},{1,17},{... | collective-permute-start | bytes 393224 | tf_op jit(solution)/shard_map/ppermute | solution.py:275
  35.5 2.9 %collective-permute-done.4 = f32[16,2048]{1,0:T(8,128)S(1)} collective-permute-done((f32[16,2048]{1,0:T(8,128)S(1)}, f32[16,2048]{1,0:T(8,128)S(1)}, u32[]{:S(2)}, u32[]{:S(2)}) %collective-permute-start.4) | collective-permute-done | bytes 131104 | tf_op jit(solution)/shard_map/ppermute | solution.py:275
  39.1 1.3 collective-permute-done.5
  40.6 5.8 %inverse_0.1 = f32[64,1024]{1,0:T(8,128)S(1)} custom-call(f32[64,2048]{1,0:T(8,128)S(1)} %pad_maximum_fusion.1.x, f32[2,1024,2048]{2,1,0:T(8,128)} %inverse.3), custom_call_target="tpu_custom_call" | custom-call | flops 805306368 | bytes 8388608 | tf_op jit(solution)/shard_map/inverse_0/pallas_call | solution.py:154
  46.4 1.8 %collective-permute-start.6 = (f32[32,1024]{1,0:T(8,128)S(1)}, f32[32,1024]{1,0:T(8,128)S(1)}, u32[]{:S(2)}, u32[]{:S(2)}) collective-permute-start(f32[32,1024]{1,0:T(8,128)S(1)} %get-tuple-element.23), channel_id=1, source_target_pairs={{0,1},{1,0},{2,3},{3,2},{4,5},{5,4},{6,7},{7,6},{8,9},{9,8},{10,11... | collective-permute-start | bytes 393224 | tf_op jit(solution)/shard_map/ppermute | solution.py:275
  48.2 2.5 %collective-permute-start.8 = (f32[32,1024]{1,0:T(8,128)S(1)}, f32[32,1024]{1,0:T(8,128)S(1)}, u32[]{:S(2)}, u32[]{:S(2)}) collective-permute-start(f32[32,1024]{1,0:T(8,128)S(1)} %get-tuple-element.24), channel_id=1, source_target_pairs={{0,3},{1,2},{2,1},{3,0},{4,7},{5,6},{6,5},{7,4},{8,11},{9,10},{10,... | collective-permute-start | bytes 393224 | tf_op jit(solution)/shard_map/ppermute | solution.py:275
  50.7 16.7 %prior_later.1.carry = f32[64,2048]{1,0:T(8,128)S(1)} custom-call(s32[16]{0:T(128)S(1)} %get-tuple-element.30.order, s32[4]{0:T(128)S(1)} %pad_add_fusion.place, f32[8,4096]{1,0:T(8,128)S(1)} %copy-done.5, f32[1,4096]{1,0:T(1,128)S(1)} %bitcast.41, bf16[64,4096]{1,0:T(8,128)(2,1)S(1)} %copy-done.3, f32[8,4096]{1,0:T(8,128)S(1)} %copy-done.1, ...), custom_call_target="tpu_custom_call" | custom-call | flops 2264924160 | bytes 1048576 | tf_op jit(solution)/shard_map/prior_later/pallas_call | solution.py:114
  69.1 17.7 %all-gather = f32[32,4096]{1,0:T(8,128)S(1)} all-gather(f32[8,4096]{1,0:T(8,128)S(1)} %copy-done.1), channel_id=2, replica_groups=mesh['wide'=8,'narrow'=4] {'narrow'}, dimensions={0}, use_global_device_ids=true | all-gather | bytes 655360 | tf_op jit(solution)/shard_map/all_gather | solution.py:369
  86.9 8.3 %kernel_0_next.1 = f32[64,2048]{1,0:T(8,128)S(1)} custom-call(s32[16]{0:T(128)S(1)} %get-tuple-element.30.order, s32[8]{0:T(128)S(1)} %get-tuple-element.31.rows, s32[4]{0:T(128)S(1)} %pad_add_fusion.place, f32[4,8,4096]{2,1,0:T(8,128)S(1)} %bitcast.37, f32[8,1]{1,0:T(8,128)S(1)} %copy.13.scales, f32[64,1024]{1,0:T(8,128)S(1)} %get-tuple-element.10.update, ...), custom_call_target="tpu_custom_call" | custom-call | flops 1086324736 | bytes 1048576 | tf_op jit(solution)/shard_map/kernel_0_next/pallas_call | solution.py:245
  95.4 1.5 collective-permute-done.10
  97.0 1.6 collective-permute-start.11
  98.5 1.5 collective-permute-start.13
  100.1 2.5 %collective-permute-done.11 = f32[16,2048]{1,0:T(8,128)S(1)} collective-permute-done((f32[16,2048]{1,0:T(8,128)S(1)}, f32[16,2048]{1,0:T(8,128)S(1)}, u32[]{:S(2)}, u32[]{:S(2)}) %collective-permute-start.11) | collective-permute-done | bytes 131104 | tf_op jit(solution)/shard_map/ppermute | solution.py:275
  104.4 1.5 collective-permute-start.12
  105.9 2.9 %collective-permute-done.14 = f32[16,2048]{1,0:T(8,128)S(1)} collective-permute-done((f32[16,2048]{1,0:T(8,128)S(1)}, f32[16,2048]{1,0:T(8,128)S(1)}, u32[]{:S(2)}, u32[]{:S(2)}) %collective-permute-start.14) | collective-permute-done | bytes 131104 | tf_op jit(solution)/shard_map/ppermute | solution.py:275
  109.5 1.5 collective-permute-done.15
  111.1 5.8 %inverse_1.1 = f32[64,1024]{1,0:T(8,128)S(1)} custom-call(f32[64,2048]{1,0:T(8,128)S(1)} %pad_maximum_fusion.2.x, f32[2,1024,2048]{2,1,0:T(8,128)} %inverse.3), custom_call_target="tpu_custom_call" | custom-call | flops 805306368 | bytes 8388608 | tf_op jit(solution)/shard_map/inverse_1/pallas_call | solution.py:154
  117.6 2.1 %collective-permute-start.18 = (f32[32,1024]{1,0:T(8,128)S(1)}, f32[32,1024]{1,0:T(8,128)S(1)}, u32[]{:S(2)}, u32[]{:S(2)}) collective-permute-start(f32[32,1024]{1,0:T(8,128)S(1)} %get-tuple-element.16), channel_id=1, source_target_pairs={{0,3},{1,2},{2,1},{3,0},{4,7},{5,6},{6,5},{7,4},{8,11},{9,10},{10,... | collective-permute-start | bytes 393224 | tf_op jit(solution)/shard_map/ppermute | solution.py:275
  119.7 8.3 %kernel_0_own.1 = f32[64,2048]{1,0:T(8,128)S(1)} custom-call(s32[16]{0:T(128)S(1)} %get-tuple-element.29.order, s32[8]{0:T(128)S(1)} %get-tuple-element.31.rows, s32[4]{0:T(128)S(1)} %pad_add_fusion.place, f32[4,8,4096]{2,1,0:T(8,128)S(1)} %bitcast.38, f32[8,1]{1,0:T(8,128)S(1)} %copy.13.scales, f32[64,1024]{1,0:T(8,128)S(1)} %get-tuple-element.10.update, ...), custom_call_target="tpu_custom_call" | custom-call | flops 1086324736 | bytes 1048576 | tf_op jit(solution)/shard_map/kernel_0_own/pallas_call | solution.py:245
  129.3 1.3 collective-permute-start.17
  130.6 3.4 %collective-permute-done.19 = f32[32,1024]{1,0:T(8,128)S(1)} collective-permute-done((f32[32,1024]{1,0:T(8,128)S(1)}, f32[32,1024]{1,0:T(8,128)S(1)}, u32[]{:S(2)}, u32[]{:S(2)}) %collective-permute-start.19) | collective-permute-done | bytes 131104 | tf_op jit(solution)/shard_map/ppermute | solution.py:275
  134.0 2.3 %collective-permute-done.17 = f32[32,1024]{1,0:T(8,128)S(1)} collective-permute-done((f32[32,1024]{1,0:T(8,128)S(1)}, f32[32,1024]{1,0:T(8,128)S(1)}, u32[]{:S(2)}, u32[]{:S(2)}) %collective-permute-start.17) | collective-permute-done | bytes 131104 | tf_op jit(solution)/shard_map/ppermute | solution.py:275
  136.4 15.7 %kernel_1.1 = f32[8,64,512]{2,1,0:T(8,128)S(1)} custom-call(s32[32]{0:T(128)S(1)} %reshape.12.order, s32[8]{0:T(128)S(1)} %get-tuple-element.32.rows, s32[4]{0:T(128)S(1)} %pad_add_fusion.place, f32[4,8,4096]{2,1,0:T(8,128)S(1)} %bitcast.39, f32[8,1]{1,0:T(8,128)S(1)} %copy.13.scales, f32[64,1024]{1,0:T(8,128)S(1)} %get-tuple-element.12.update, ...), custom_call_target="tpu_custom_call" | custom-call | flops 2172649472 | bytes 2097152 | tf_op jit(solution)/shard_map/kernel_1/pallas_call | solution.py:245
  152.3 1.9 %collective-permute-done.20 = f32[4,64,512]{2,1,0:T(8,128)S(1)} collective-permute-done((f32[4,64,512]{2,1,0:T(8,128)S(1)}, f32[4,64,512]{2,1,0:T(8,128)S(1)}, u32[]{:S(2)}, u32[]{:S(2)}) %collective-permute-start.20) | collective-permute-done | bytes 524320 | tf_op jit(solution)/shard_map/ppermute | solution.py:275
  154.3 2.5 %collective-permute-start.23 = (f32[64,512]{1,0:T(8,128)S(1)}, f32[64,512]{1,0:T(8,128)S(1)}, u32[]{:S(2)}, u32[]{:S(2)}) collective-permute-start(f32[64,512]{1,0:T(8,128)S(1)} %get-tuple-element.3), channel_id=1, source_target_pairs={{0,24},{4,28},{8,16},{12,20},{16,8},{20,12},{24,0},{28,4},{1,25},{... | collective-permute-start | bytes 393224 | tf_op jit(solution)/shard_map/ppermute | solution.py:275
  158.6 2.4 %collective-permute-done.23 = f32[64,512]{1,0:T(8,128)S(1)} collective-permute-done((f32[64,512]{1,0:T(8,128)S(1)}, f32[64,512]{1,0:T(8,128)S(1)}, u32[]{:S(2)}, u32[]{:S(2)}) %collective-permute-start.23) | collective-permute-done | bytes 131104 | tf_op jit(solution)/shard_map/ppermute | solution.py:275
  161.0 2.5 %collective-permute-done.22 = f32[64,512]{1,0:T(8,128)S(1)} collective-permute-done((f32[64,512]{1,0:T(8,128)S(1)}, f32[64,512]{1,0:T(8,128)S(1)}, u32[]{:S(2)}, u32[]{:S(2)}) %collective-permute-start.22) | collective-permute-done | bytes 131104 | tf_op jit(solution)/shard_map/ppermute | solution.py:275
  (91 shorter events, 18.4 us)
Async XLA Ops:
  0.6 38.3 %copy-start.11 = (s32[2,64]{1,0:T(2,128)S(1)}, s32[2,64]{1,0:T(2,128)}, u32[]{:S(2)}) copy-start(s32[2,64]{1,0:T(2,128)} %param.17) | copy-start | bytes 1540
  0.6 38.4 %copy-start.12 = (f32[8]{0:T(128)S(1)}, f32[8]{0:T(128)}, u32[]{:S(2)}) copy-start(f32[8]{0:T(128)} %param.10) | copy-start | bytes 100
  2.4 1.0 copy-start.2
  6.7 44.0 %copy-start.1 = (f32[8,4096]{1,0:T(8,128)S(1)}, f32[8,4096]{1,0:T(8,128)}, u32[]{:S(2)}) copy-start(f32[8,4096]{1,0:T(8,128)} %points.3) | copy-start | bytes 393220
  6.7 44.0 %copy-start.3 = (bf16[64,4096]{1,0:T(8,128)(2,1)S(1)}, bf16[64,4096]{1,0:T(8,128)(2,1)}, u32[]{:S(2)}) copy-start(bf16[64,4096]{1,0:T(8,128)(2,1)} %fw.3) | copy-start | bytes 1572868
  6.7 44.0 %copy-start.5 = (f32[8,4096]{1,0:T(8,128)S(1)}, f32[8,4096]{1,0:T(8,128)}, u32[]{:S(2)}) copy-start(f32[8,4096]{1,0:T(8,128)} %freq.3) | copy-start | bytes 393220
  6.7 44.0 %copy-start.8 = (f32[4096]{0:T(1024)S(1)}, f32[4096]{0:T(1024)}, u32[]{:S(2)}) copy-start(f32[4096]{0:T(1024)} %param.12) | copy-start | bytes 49156
  6.7 44.0 %copy-start.10 = (f32[512]{0:T(512)S(1)}, f32[512]{0:T(512)}, u32[]{:S(2)}) copy-start(f32[512]{0:T(512)} %param.14) | copy-start | bytes 6148
  23.5 1.7 %collective-permute-start = (f32[32,2048]{1,0:T(8,128)S(1)}, f32[32,2048]{1,0:T(8,128)S(1)}, u32[]{:S(2)}, u32[]{:S(2)}) collective-permute-start(f32[32,2048]{1,0:T(8,128)S(1)} %constant_dynamic-slice_fusion.1), channel_id=1, source_target_pairs={{0,4},{4,0},{8,12},{12,8},{16,20},{20,16},{24,28},{28,24},{1,5},{5... | collective-permute-start | bytes 786440 | tf_op jit(solution)/shard_map/ppermute | solution.py:275
  25.2 6.7 %collective-permute-start.1 = (f32[16,2048]{1,0:T(8,128)S(1)}, f32[16,2048]{1,0:T(8,128)S(1)}, u32[]{:S(2)}, u32[]{:S(2)}) collective-permute-start(f32[16,2048]{1,0:T(8,128)S(1)} %get-tuple-element.27), channel_id=1, source_target_pairs={{0,8},{4,12},{8,0},{12,4},{16,24},{20,28},{24,16},{28,20},{1,9},{5... | collective-permute-start | bytes 393224 | tf_op jit(solution)/shard_map/ppermute | solution.py:275
  28.1 5.3 %collective-permute-start.3 = (f32[16,2048]{1,0:T(8,128)S(1)}, f32[16,2048]{1,0:T(8,128)S(1)}, u32[]{:S(2)}, u32[]{:S(2)}) collective-permute-start(f32[16,2048]{1,0:T(8,128)S(1)} %get-tuple-element.28), channel_id=1, source_target_pairs={{0,16},{4,20},{8,24},{12,28},{16,0},{20,4},{24,8},{28,12},{1,17},{... | collective-permute-start | bytes 393224 | tf_op jit(solution)/shard_map/ppermute | solution.py:275
  33.4 5.0 %collective-permute-start.4 = (f32[16,2048]{1,0:T(8,128)S(1)}, f32[16,2048]{1,0:T(8,128)S(1)}, u32[]{:S(2)}, u32[]{:S(2)}) collective-permute-start(f32[16,2048]{1,0:T(8,128)S(1)} %get-tuple-element.26), channel_id=1, source_target_pairs={{0,8},{4,12},{8,0},{12,4},{16,24},{20,28},{24,16},{28,20},{1,9},{5... | collective-permute-start | bytes 393224 | tf_op jit(solution)/shard_map/ppermute | solution.py:275
  33.8 5.0 %collective-permute-start.2 = (f32[16,2048]{1,0:T(8,128)S(1)}, f32[16,2048]{1,0:T(8,128)S(1)}, u32[]{:S(2)}, u32[]{:S(2)}) collective-permute-start(f32[16,2048]{1,0:T(8,128)S(1)} %get-tuple-element.25), channel_id=1, source_target_pairs={{0,16},{4,20},{8,24},{12,28},{16,0},{20,4},{24,8},{28,12},{1,17},{... | collective-permute-start | bytes 393224 | tf_op jit(solution)/shard_map/ppermute | solution.py:275
  38.9 1.6 collective-permute-start.5
  46.4 21.0 %collective-permute-start.6 = (f32[32,1024]{1,0:T(8,128)S(1)}, f32[32,1024]{1,0:T(8,128)S(1)}, u32[]{:S(2)}, u32[]{:S(2)}) collective-permute-start(f32[32,1024]{1,0:T(8,128)S(1)} %get-tuple-element.23), channel_id=1, source_target_pairs={{0,1},{1,0},{2,3},{3,2},{4,5},{5,4},{6,7},{7,6},{8,9},{9,8},{10,11... | collective-permute-start | bytes 393224 | tf_op jit(solution)/shard_map/ppermute | solution.py:275
  48.2 19.2 %collective-permute-start.8 = (f32[32,1024]{1,0:T(8,128)S(1)}, f32[32,1024]{1,0:T(8,128)S(1)}, u32[]{:S(2)}, u32[]{:S(2)}) collective-permute-start(f32[32,1024]{1,0:T(8,128)S(1)} %get-tuple-element.24), channel_id=1, source_target_pairs={{0,3},{1,2},{2,1},{3,0},{4,7},{5,6},{6,5},{7,4},{8,11},{9,10},{10,... | collective-permute-start | bytes 393224 | tf_op jit(solution)/shard_map/ppermute | solution.py:275
  67.5 19.4 %collective-permute-start.9 = (f32[32,1024]{1,0:T(8,128)S(1)}, f32[32,1024]{1,0:T(8,128)S(1)}, u32[]{:S(2)}, u32[]{:S(2)}) collective-permute-start(f32[32,1024]{1,0:T(8,128)S(1)} %get-tuple-element.22), channel_id=1, source_target_pairs={{0,1},{1,0},{2,3},{3,2},{4,5},{5,4},{6,7},{7,6},{8,9},{9,8},{10,11... | collective-permute-start | bytes 393224 | tf_op jit(solution)/shard_map/ppermute | solution.py:275
  68.2 18.7 %collective-permute-start.7 = (f32[32,1024]{1,0:T(8,128)S(1)}, f32[32,1024]{1,0:T(8,128)S(1)}, u32[]{:S(2)}, u32[]{:S(2)}) collective-permute-start(f32[32,1024]{1,0:T(8,128)S(1)} %get-tuple-element.21), channel_id=1, source_target_pairs={{0,3},{1,2},{2,1},{3,0},{4,7},{5,6},{6,5},{7,4},{8,11},{9,10},{10,... | collective-permute-start | bytes 393224 | tf_op jit(solution)/shard_map/ppermute | solution.py:275
  95.3 1.6 collective-permute-start.10
  97.0 5.6 %collective-permute-start.11 = (f32[16,2048]{1,0:T(8,128)S(1)}, f32[16,2048]{1,0:T(8,128)S(1)}, u32[]{:S(2)}, u32[]{:S(2)}) collective-permute-start(f32[16,2048]{1,0:T(8,128)S(1)} %get-tuple-element.19), channel_id=1, source_target_pairs={{0,8},{4,12},{8,0},{12,4},{16,24},{20,28},{24,16},{28,20},{1,9},{5... | collective-permute-start | bytes 393224 | tf_op jit(solution)/shard_map/ppermute | solution.py:275
  98.5 5.3 %collective-permute-start.13 = (f32[16,2048]{1,0:T(8,128)S(1)}, f32[16,2048]{1,0:T(8,128)S(1)}, u32[]{:S(2)}, u32[]{:S(2)}) collective-permute-start(f32[16,2048]{1,0:T(8,128)S(1)} %get-tuple-element.20), channel_id=1, source_target_pairs={{0,16},{4,20},{8,24},{12,28},{16,0},{20,4},{24,8},{28,12},{1,17},{... | collective-permute-start | bytes 393224 | tf_op jit(solution)/shard_map/ppermute | solution.py:275
  103.8 5.0 %collective-permute-start.14 = (f32[16,2048]{1,0:T(8,128)S(1)}, f32[16,2048]{1,0:T(8,128)S(1)}, u32[]{:S(2)}, u32[]{:S(2)}) collective-permute-start(f32[16,2048]{1,0:T(8,128)S(1)} %get-tuple-element.18), channel_id=1, source_target_pairs={{0,8},{4,12},{8,0},{12,4},{16,24},{20,28},{24,16},{28,20},{1,9},{5... | collective-permute-start | bytes 393224 | tf_op jit(solution)/shard_map/ppermute | solution.py:275
  104.4 5.0 %collective-permute-start.12 = (f32[16,2048]{1,0:T(8,128)S(1)}, f32[16,2048]{1,0:T(8,128)S(1)}, u32[]{:S(2)}, u32[]{:S(2)}) collective-permute-start(f32[16,2048]{1,0:T(8,128)S(1)} %get-tuple-element.17), channel_id=1, source_target_pairs={{0,16},{4,20},{8,24},{12,28},{16,0},{20,4},{24,8},{28,12},{1,17},{... | collective-permute-start | bytes 393224 | tf_op jit(solution)/shard_map/ppermute | solution.py:275
  109.5 1.6 collective-permute-start.15
  117.0 11.1 %collective-permute-start.16 = (f32[32,1024]{1,0:T(8,128)S(1)}, f32[32,1024]{1,0:T(8,128)S(1)}, u32[]{:S(2)}, u32[]{:S(2)}) collective-permute-start(f32[32,1024]{1,0:T(8,128)S(1)} %get-tuple-element.15), channel_id=1, source_target_pairs={{0,1},{1,0},{2,3},{3,2},{4,5},{5,4},{6,7},{7,6},{8,9},{9,8},{10,11... | collective-permute-start | bytes 393224 | tf_op jit(solution)/shard_map/ppermute | solution.py:275
  117.6 10.5 %collective-permute-start.18 = (f32[32,1024]{1,0:T(8,128)S(1)}, f32[32,1024]{1,0:T(8,128)S(1)}, u32[]{:S(2)}, u32[]{:S(2)}) collective-permute-start(f32[32,1024]{1,0:T(8,128)S(1)} %get-tuple-element.16), channel_id=1, source_target_pairs={{0,3},{1,2},{2,1},{3,0},{4,7},{5,6},{6,5},{7,4},{8,11},{9,10},{10,... | collective-permute-start | bytes 393224 | tf_op jit(solution)/shard_map/ppermute | solution.py:275
  128.1 5.8 %collective-permute-start.19 = (f32[32,1024]{1,0:T(8,128)S(1)}, f32[32,1024]{1,0:T(8,128)S(1)}, u32[]{:S(2)}, u32[]{:S(2)}) collective-permute-start(f32[32,1024]{1,0:T(8,128)S(1)} %get-tuple-element.14), channel_id=1, source_target_pairs={{0,1},{1,0},{2,3},{3,2},{4,5},{5,4},{6,7},{7,6},{8,9},{9,8},{10,11... | collective-permute-start | bytes 393224 | tf_op jit(solution)/shard_map/ppermute | solution.py:275
  129.3 7.1 %collective-permute-start.17 = (f32[32,1024]{1,0:T(8,128)S(1)}, f32[32,1024]{1,0:T(8,128)S(1)}, u32[]{:S(2)}, u32[]{:S(2)}) collective-permute-start(f32[32,1024]{1,0:T(8,128)S(1)} %get-tuple-element.13), channel_id=1, source_target_pairs={{0,3},{1,2},{2,1},{3,0},{4,7},{5,6},{6,5},{7,4},{8,11},{9,10},{10,... | collective-permute-start | bytes 393224 | tf_op jit(solution)/shard_map/ppermute | solution.py:275
  152.1 2.0 %collective-permute-start.20 = (f32[4,64,512]{2,1,0:T(8,128)S(1)}, f32[4,64,512]{2,1,0:T(8,128)S(1)}, u32[]{:S(2)}, u32[]{:S(2)}) collective-permute-start(f32[4,64,512]{2,1,0:T(8,128)S(1)} %dynamic-slice_bitcast_fusion), channel_id=1, source_target_pairs={{0,4},{4,0},{8,12},{12,8},{16,20},{20,16},{24,28},{28,24},{1,5},{5... | collective-permute-start | bytes 1572872 | tf_op jit(solution)/shard_map/ppermute | solution.py:275
  154.3 6.8 %collective-permute-start.23 = (f32[64,512]{1,0:T(8,128)S(1)}, f32[64,512]{1,0:T(8,128)S(1)}, u32[]{:S(2)}, u32[]{:S(2)}) collective-permute-start(f32[64,512]{1,0:T(8,128)S(1)} %get-tuple-element.3), channel_id=1, source_target_pairs={{0,24},{4,28},{8,16},{12,20},{16,8},{20,12},{24,0},{28,4},{1,25},{... | collective-permute-start | bytes 393224 | tf_op jit(solution)/shard_map/ppermute | solution.py:275
  156.8 6.8 %collective-permute-start.22 = (f32[64,512]{1,0:T(8,128)S(1)}, f32[64,512]{1,0:T(8,128)S(1)}, u32[]{:S(2)}, u32[]{:S(2)}) collective-permute-start(f32[64,512]{1,0:T(8,128)S(1)} %get-tuple-element.4), channel_id=1, source_target_pairs={{0,16},{4,20},{8,24},{12,28},{16,0},{20,4},{24,8},{28,12},{1,17},{... | collective-permute-start | bytes 393224 | tf_op jit(solution)/shard_map/ppermute | solution.py:275
  157.3 6.4 %collective-permute-start.21 = (f32[64,512]{1,0:T(8,128)S(1)}, f32[64,512]{1,0:T(8,128)S(1)}, u32[]{:S(2)}, u32[]{:S(2)}) collective-permute-start(f32[64,512]{1,0:T(8,128)S(1)} %get-tuple-element.2), channel_id=1, source_target_pairs={{0,8},{4,12},{8,0},{12,4},{16,24},{20,28},{24,16},{28,20},{1,9},{5... | collective-permute-start | bytes 393224 | tf_op jit(solution)/shard_map/ppermute | solution.py:275
  (5 other events, 4.1 us)
